TPU v7x, 512 devices: a whole 4x4x16 slice. The times are simulated.
512 devices in a mesh: side: 2 (over y_lo), gx: 32 (over y_hi, z), gy: 8 (over x, core).
Axes of the slice: x: 4, y: 4 (y_hi: 2, y_lo: 2; y = y_hi * 2 + y_lo), z: 16, core: 2. Of those that a mesh axis runs over, the one named last changes fastest.
Arguments:
- hidden_in: bfloat16 [32, 2, 8192], P(None, None, ('side', 'gx')), may hold values from -10 to 10
- queries: bfloat16 [32, 2, 64, 128], P('gx', None, 'gy'), may hold values from -110 to 110
- kv_cache: bfloat16 [32, 2048, 8, 256], P('gx', 'side', 'gy'), may hold values from -6 to 6
- new_kv: bfloat16 [32, 2, 8, 256], P('gx', None, 'gy'), may hold values from -5 to 5
- lengths: int32 [32], P('gx'), may hold values from 256 to 2048
- out_weight: bfloat16 [8192, 8192], P('gy', ('side', 'gx')), may hold values from -1 to 1
- norm_gain: float32 [8192], P(('side', 'gx')), may hold values from 0.5 to 1.5
- gate_weight: bfloat16 [8192, 28672], P(('side', 'gx'), 'gy'), may hold values from -0.0625 to 0.0625
- up_weight: bfloat16 [8192, 28672], P(('side', 'gx'), 'gy'), may hold values from -0.0625 to 0.0625
- down_weight: bfloat16 [28672, 8192], P('gy', ('side', 'gx')), may hold values from -0.03125 to 0.03125
Outputs:
- hidden_out: bfloat16 [32, 2, 8192], P(None, None, ('side', 'gx'))
All inputs are finite; a program needn't handle non-finite values.
Results may differ from a plain program's by a relative error of at most 0.014.
Values may be sent and summed in bfloat16 or wider, within the bound.
No kernel may reach another device: no remote copies, remote signals or barrier semaphores. Data moves between devices by JAX's collectives and lax.ppermute only.
A program may use at most 64 MiB of HBM per device.

v0:
```python
import math

import jax
import jax.numpy as jnp
from jax import lax
from jax.sharding import PartitionSpec as P

D = 8192


big_negative = -1e30


def merged(value, axis, combine):
    everything = jax.tree.map(lambda part: lax.all_gather(part, axis), value)
    initial = jax.tree.map(lambda part: part[0], everything)

    def turn(k, so_far):
        return combine(so_far, jax.tree.map(lambda part: part[k], everything))

    return lax.fori_loop(1, lax.axis_size(axis), turn, initial)


def merge_parts(first, second):
    peak_a, total_a, accum_a = first
    peak_b, total_b, accum_b = second
    peak = jnp.maximum(peak_a, peak_b)
    factor_a = jnp.exp(peak_a - peak)
    factor_b = jnp.exp(peak_b - peak)
    return (
        peak,
        total_a * factor_a + total_b * factor_b,
        accum_a * factor_a[..., None] + accum_b * factor_b[..., None],
    )


def partial_attention(queries, kv_cache, new_kv, lengths, side_index, last_side):
    requests, half, kv_heads, doubled = kv_cache.shape
    head_size = doubled // 2
    group = queries.shape[2] // kv_heads
    query = jnp.transpose(queries.reshape(requests, 2, kv_heads, group, head_size), (0, 2, 1, 3, 4))
    query = query.reshape(requests, kv_heads, 2 * group, head_size)
    scores = jnp.einsum(
        "bgrd,bcgd->bgrc", query, kv_cache[..., :head_size], preferred_element_type=jnp.float32
    ) / math.sqrt(head_size)
    position = side_index * half + lax.iota(jnp.int32, half)
    usable = (position[None, :] < lengths[:, None])[:, None, None, :]
    peak = jnp.max(jnp.where(usable, scores, big_negative), axis=-1)
    weights = jnp.where(usable, jnp.exp(scores - peak[..., None]), 0.0)
    accum = jnp.einsum(
        "bgrc,bcgd->bgrd",
        weights.astype(jnp.bfloat16),
        kv_cache[..., head_size:],
        preferred_element_type=jnp.float32,
    )
    fresh = jnp.einsum(
        "bgrd,btgd->bgrt", query, new_kv[..., :head_size], preferred_element_type=jnp.float32
    ) / math.sqrt(head_size)
    draft = lax.iota(jnp.int32, 2 * group) // group
    seen = (lax.iota(jnp.int32, 2)[None, :] <= draft[:, None]) & last_side
    fresh_peak = jnp.max(jnp.where(seen, fresh, big_negative), axis=-1)
    fresh_weights = jnp.where(seen, jnp.exp(fresh - fresh_peak[..., None]), 0.0)
    fresh_accum = jnp.einsum(
        "bgrt,btgd->bgrd",
        fresh_weights.astype(jnp.bfloat16),
        new_kv[..., head_size:],
        preferred_element_type=jnp.float32,
    )
    own = (peak, jnp.sum(weights, axis=-1), accum)
    return merge_parts(own, (fresh_peak, jnp.sum(fresh_weights, axis=-1), fresh_accum))


def to_rows(parts, kv_heads, width):
    peak, total, accum = parts
    count, rows_group, head_size = (accum.shape[0], accum.shape[2], accum.shape[3])
    mixed = (accum / total[..., None]).astype(jnp.bfloat16)
    mixed = mixed.reshape(count, kv_heads, 2, rows_group // 2, head_size)
    return jnp.transpose(mixed, (0, 2, 1, 3, 4)).reshape(count * 2, width)


def local(
    hidden_in,
    queries,
    kv_cache,
    new_kv,
    lengths,
    out_weight,
    norm_gain,
    gate_weight,
    up_weight,
    down_weight,
):
    side_index = lax.axis_index("side")
    last_side = side_index == lax.axis_size("side") - 1
    parts = partial_attention(queries, kv_cache, new_kv, lengths, side_index, last_side)
    kv_heads = kv_cache.shape[2]
    width = out_weight.shape[0]
    joined = merged(parts, "side", merge_parts)
    local_rows = to_rows(joined, kv_heads, width)
    attn_part = jnp.dot(
        lax.all_gather(local_rows, "gx", axis=0, tiled=True),
        out_weight,
        preferred_element_type=jnp.float32,
    )
    attn_sum = lax.psum(attn_part.astype(jnp.bfloat16), "gy").astype(jnp.float32)
    rows_all = attn_sum.shape[0]
    middle = hidden_in.reshape(rows_all, -1).astype(jnp.float32) + attn_sum
    squares = lax.psum(jnp.sum(middle * middle, axis=1), ("side", "gx"))
    normed = (middle * lax.rsqrt(squares / D + 1e-05)[:, None] * norm_gain).astype(jnp.bfloat16)
    gate_term = jnp.dot(normed, gate_weight, preferred_element_type=jnp.float32)
    up_term = jnp.dot(normed, up_weight, preferred_element_type=jnp.float32)
    gate_sum, up_sum = lax.psum((gate_term, up_term), ("side", "gx"))
    activated = (jax.nn.silu(gate_sum) * up_sum).astype(jnp.bfloat16)
    ffn_part = jnp.dot(activated, down_weight, preferred_element_type=jnp.float32)
    ffn_sum = lax.psum(ffn_part.astype(jnp.bfloat16), "gy").astype(jnp.float32)
    return (middle + ffn_sum).astype(jnp.bfloat16).reshape(hidden_in.shape)


def solution(mesh):
    in_specs = (
        P(None, None, ("side", "gx")),
        P("gx", None, "gy", None),
        P("gx", "side", "gy", None),
        P("gx", None, "gy", None),
        P("gx"),
        P("gy", ("side", "gx")),
        P(("side", "gx")),
        P(("side", "gx"), "gy"),
        P(("side", "gx"), "gy"),
        P("gy", ("side", "gx")),
    )
    out_specs = P(None, None, ("side", "gx"))
    return jax.shard_map(local, mesh=mesh, in_specs=in_specs, out_specs=out_specs, check_vma=False)
```

profile of v0, /device:TPU:1, one launch (start us, length us, event | category | flops | bytes accessed | tf_op | source)
XLA Modules:
  0.0 574.0 jit_solution(5062571026604150591)
XLA Ops:
  6.5 0.0 copy-start
  6.5 0.0 all-reduce.3.cloned.1.call-start
  7.3 0.0 copy-start.7
  7.3 0.0 copy-done.4
  7.3 0.6 copy-done.7
  8.0 0.1 select_reduce_fusion.1
  8.1 1.2 select_reduce_fusion
  9.4 0.2 fusion.5
  9.6 3.7 all_gather.19
  13.3 3.1 all_gather.20
  16.4 1.2 convolution_multiply_fusion.2
  17.6 0.1 div.49
  17.6 0.1 fusion
  17.8 3.3 all-gather
  21.1 0.1 mul.130
  21.2 0.1 mul.133
  21.3 69.5 %all-gather.1 = bf16[32,2,1024]{2,1,0:T(2,128)(2,1)S(1)} all-gather(bf16[1,2,1024]{2,1,0:T(2,128)(2,1)S(1)} %fusion.14), channel_id=1, replica_groups=mesh['side'=2,'gx'=32,'gy'=8] {'gx'}, dimensions={0}, use_global_device_ids=true | all-gather | bytes 135168 | tf_op jit(solution)/shard_map/all_gather | solution.py:101
  90.8 0.1 reshape.300
  90.9 0.2 convolution_convert_fusion.1
  91.0 0.0 copy-start.2
  91.1 38.0 %psum.35 = bf16[64,128]{1,0:T(8,128)(2,1)S(1)} all-reduce(bf16[64,128]{1,0:T(8,128)(2,1)S(1)} %convolution_convert_fusion.1), channel_id=1, replica_groups=mesh['side'=2,'gx'=32,'gy'=8] {'gy'}, use_global_device_ids=true, to_apply=%region_4.5 | all-reduce | flops 8192 | bytes 32768 | tf_op jit(solution)/shard_map/psum | solution.py:105
  129.1 0.0 copy-done.2
  129.1 0.1 multiply_reduce_fusion
  129.2 110.5 %psum.36 = f32[64]{0:T(128)S(1)} all-reduce(f32[64]{0:T(128)S(1)} %multiply_reduce_fusion), channel_id=1, replica_groups=mesh['side'=2,'gx'=32,'gy'=8] {'side','gx'}, use_global_device_ids=true, to_apply=%region_6.7 | all-reduce | flops 64 | bytes 512 | tf_op jit(solution)/shard_map/psum | solution.py:108
  239.7 0.6 copy-done.5
  240.3 1.3 fusion.33
  241.6 1.3 fusion.34
  242.9 0.0 all-reduce.3.cloned.1.call-update
  242.9 292.1 %all-reduce.3.cloned.1.call-done = (f32[64,3584]{1,0:T(8,128)}, f32[64,3584]{1,0:T(8,128)}) async-done(((f32[64,3584]{1,0:T(8,128)}, f32[64,3584]{1,0:T(8,128)}), (f32[64,3584]{1,0:T(8,128)}, f32[64,3584]{1,0:T(8,128)})) %all-reduce.3.cloned.1.call-update) | async-done | bytes 1835024 | tf_op jit(solution)/shard_map/psum | solution.py:112
  535.1 1.8 convolution_convert_fusion
  536.9 29.7 %psum.39 = bf16[64,128]{1,0:T(8,128)(2,1)S(1)} all-reduce(bf16[64,128]{1,0:T(8,128)(2,1)S(1)} %convolution_convert_fusion), channel_id=1, replica_groups=mesh['side'=2,'gx'=32,'gy'=8] {'gy'}, use_global_device_ids=true, to_apply=%region_9.10 | all-reduce | flops 8192 | bytes 32768 | tf_op jit(solution)/shard_map/psum | solution.py:115
  566.6 0.6 add_convert_fusion
  (23 shorter events, 0.2 us)
Async XLA Ops:
  6.5 233.2 %copy-start = (bf16[128,3584]{1,0:T(8,128)(2,1)S(1)}, bf16[128,3584]{1,0:T(8,128)(2,1)}, u32[]{:S(2)}) copy-start(bf16[128,3584]{1,0:T(8,128)(2,1)} %param.18) | copy-start | bytes 2752516
  6.5 528.5 %all-reduce.3.cloned.1.call-start = ((), (), s32[]{:S(2)}) async-start(), calls=%async_computation | async-start | bytes 3670016 | tf_op jit(solution)/shard_map/psum | solution.py:112
  6.5 0.8 copy-start.4
  7.3 0.7 copy-start.7
  21.0 69.8 %copy-start.3 = (bf16[1024,128]{1,0:T(8,128)(2,1)S(1)}, bf16[1024,128]{1,0:T(8,128)(2,1)}, u32[]{:S(2)}) copy-start(bf16[1024,128]{1,0:T(8,128)(2,1)} %param.15) | copy-start | bytes 786436
  91.0 38.0 %copy-start.2 = (bf16[32,2,128]{2,1,0:T(2,128)(2,1)S(1)}, bf16[32,2,128]{2,1,0:T(2,128)(2,1)}, u32[]{:S(2)}) copy-start(bf16[32,2,128]{2,1,0:T(2,128)(2,1)} %param.10) | copy-start | bytes 49156
  239.7 0.7 copy-start.5
  240.3 1.3 copy-start.1
  242.9 292.2 %copy-start.6 = (bf16[3584,128]{1,0:T(8,128)(2,1)S(1)}, bf16[3584,128]{1,0:T(8,128)(2,1)}, u32[]{:S(2)}) copy-start(bf16[3584,128]{1,0:T(8,128)(2,1)} %param.19) | copy-start | bytes 2752516
Sparse Core Ops, SparseCore 0:
  243.0 291.9 all-reduce.2
where the time goes:
time: 576 us; the launch traced here: 574 us
  waiting for transfers between devices  292 us (51%)
  blocking collectives  258 us (45%)
  between operations  14.2 us (2%)
  matrix products  7.22 us (1%)
    psum x1, waiting for transfers between devices, local(): gate_sum, up_sum = lax.psum((gate_term, up_term), ('side', 'gx'))  292 us
    psum x1, blocking collectives, local(): squares = lax.psum(jnp.sum(middle * middle, axis=1), ('side', 'gx'))  111 us
    all_gather x1, blocking collectives, local(): lax.all_gather(local_rows, 'gx', axis=0, tiled=True)  69.5 us
    psum x1, blocking collectives, local(): lax.psum(attn_part.astype(jnp.bfloat16), 'gy').astype(jnp.float32)  38 us
    psum x1, blocking collectives, local(): ffn_sum = lax.psum(ffn_part.astype(jnp.bfloat16), 'gy').astype(jnp.float32)  29.7 us
  transfers between devices with their start and end apart: 1, of which 1 were waited for; matrix products, arithmetic and copies ran while one was open for 0% of the time, Pallas kernels for 0%

commit v1 on v0

v1 whole, which is shorter than its diff:
```python
import math

import jax
import jax.numpy as jnp
from jax import lax
from jax.sharding import Mesh, PartitionSpec as P

D = 8192
big_negative = -1e30
bf16 = jnp.bfloat16
f32 = jnp.float32

SIDES, YHI, ZS = 2, 2, 16
YS = SIDES * YHI
ROWS = ("side", "yhi", "z")
Y = ("side", "yhi")
GY = ("x", "core")


def spread(value, axes, count):
    return lax.all_to_all(jnp.broadcast_to(value, (count, *value.shape)), axes, 0, 0)


def partial_attention(queries, kv_cache, new_kv, lengths, side_index, last_side):
    half, doubled = kv_cache.shape[1], kv_cache.shape[3]
    head = doubled // 2
    group = queries.shape[2]
    query = queries.reshape(2 * group, head)
    cache, fresh = kv_cache[0, :, 0], new_kv[0, :, 0]
    scale = 1.0 / math.sqrt(head)
    contract_last = (((1,), (1,)), ((), ()))
    scores = lax.dot_general(query, cache[:, :head], contract_last, preferred_element_type=f32) * scale
    usable = (side_index * half + lax.iota(jnp.int32, half) < lengths[0])[None, :]
    draft = lax.iota(jnp.int32, 2 * group) // group
    seen = (lax.iota(jnp.int32, 2)[None, :] <= draft[:, None]) & last_side
    new_scores = lax.dot_general(query, fresh[:, :head], contract_last, preferred_element_type=f32) * scale
    scores = jnp.where(usable, scores, big_negative)
    new_scores = jnp.where(seen, new_scores, big_negative)
    peak = jnp.maximum(jnp.max(scores, axis=1), jnp.max(new_scores, axis=1))
    peak = peak.astype(bf16)
    level = peak.astype(f32)[:, None]
    weights = jnp.where(usable, jnp.exp(scores - level), 0.0)
    new_weights = jnp.where(seen, jnp.exp(new_scores - level), 0.0)
    total = jnp.sum(weights, axis=1) + jnp.sum(new_weights, axis=1)
    accum = jnp.dot(weights.astype(bf16), cache[:, head:], preferred_element_type=f32)
    rounded = new_weights.astype(bf16).astype(f32)
    values = fresh[:, head:].astype(f32)
    accum = accum + rounded[:, :1] * values[:1] + rounded[:, 1:] * values[1:]
    mixed = (accum / total[:, None]).astype(bf16)
    high = total.astype(bf16)
    low = (total - high.astype(f32)).astype(bf16)
    stats = jnp.concatenate([part.reshape(2, group) for part in (peak, high, low)], axis=1)
    stats = jnp.pad(stats, ((0, 0), (0, 128 - 3 * group)))
    return jnp.concatenate([mixed.reshape(2, group * head), stats], axis=1)


def merge_sides(parts, group):
    rows = parts.shape[1]
    width = parts.shape[2] - 128
    stats = parts[:, :, width:].astype(f32)
    peak = stats[:, :, :group]
    total = stats[:, :, group : 2 * group] + stats[:, :, 2 * group : 3 * group]
    weight = total * jnp.exp(peak - jnp.max(peak, axis=0, keepdims=True))
    weight = weight / jnp.sum(weight, axis=0, keepdims=True)
    mixed = parts[:, :, :width].astype(f32).reshape(2, rows, group, width // group)
    return jnp.sum(mixed * weight[..., None], axis=0).reshape(rows, width).astype(bf16)


def local(hidden_in, queries, kv_cache, new_kv, lengths, out_weight, norm_gain, gate_weight, up_weight, down_weight):
    side_index = lax.axis_index("side")
    group = queries.shape[2]
    rows = hidden_in.shape[0] * 2
    cols = hidden_in.shape[2]
    hidden = gate_weight.shape[1]
    part = hidden // YS

    own = partial_attention(queries, kv_cache, new_kv, lengths, side_index, side_index == SIDES - 1)
    everyone = spread(own, ROWS, YS * ZS)
    attended = merge_sides(everyone.reshape(SIDES, rows, own.shape[1]), group)
    attn_part = jnp.dot(attended, out_weight, preferred_element_type=f32)
    attn_sum = jnp.sum(spread(attn_part.astype(bf16), GY, 8).astype(f32), axis=0)
    middle = hidden_in.reshape(rows, cols).astype(f32) + attn_sum

    squares = jnp.sum(middle * middle, axis=1, keepdims=True)
    scaled = (middle * norm_gain).astype(bf16)
    gate_term = jnp.dot(scaled, gate_weight, preferred_element_type=f32).astype(bf16)
    up_term = jnp.dot(scaled, up_weight, preferred_element_type=f32).astype(bf16)
    high = squares.astype(bf16)
    low = (squares - high.astype(f32)).astype(bf16)
    pair = jnp.pad(jnp.concatenate([high, low], axis=1), ((0, 0), (0, 126)))
    blocks = [
        jnp.concatenate([gate_term[:, j * part : (j + 1) * part], up_term[:, j * part : (j + 1) * part], pair], axis=1)
        for j in range(YS)
    ]
    over_y = lax.all_to_all(jnp.stack(blocks), Y, 0, 0).astype(f32)
    over_y = jnp.sum(over_y, axis=0)
    squares = over_y[:, 2 * part : 2 * part + 1] + over_y[:, 2 * part + 1 : 2 * part + 2]
    high = squares.astype(bf16)
    low = (squares - high.astype(f32)).astype(bf16)
    pair = jnp.pad(jnp.concatenate([high, low], axis=1), ((0, 0), (0, 126)))
    to_z = jnp.concatenate([over_y[:, : 2 * part].astype(bf16), pair], axis=1)
    over_z = lax.all_to_all(to_z.reshape(ZS, rows // ZS, -1), "z", 0, 0).astype(f32)
    over_z = jnp.sum(over_z, axis=0)
    squares = over_z[:, 2 * part : 2 * part + 1] + over_z[:, 2 * part + 1 : 2 * part + 2]
    factor = lax.rsqrt(squares / D + 1e-05)
    gate = over_z[:, :part] * factor
    up = over_z[:, part : 2 * part] * factor
    activated = (jax.nn.silu(gate) * up).astype(bf16)
    along_z = spread(activated, "z", ZS).reshape(rows, part)
    along_y = spread(along_z, Y, YS)
    ffn_part = sum(
        jnp.dot(along_y[j], down_weight[j * part : (j + 1) * part], preferred_element_type=f32) for j in range(YS)
    )
    ffn_sum = jnp.sum(spread(ffn_part.astype(bf16), GY, 8).astype(f32), axis=0)
    return (middle + ffn_sum).astype(bf16).reshape(hidden_in.shape)


def solution(mesh):
    fine = Mesh(mesh.devices.reshape(2, 2, 16, 4, 2), ("side", "yhi", "z", "x", "core"))
    in_specs = (
        P(None, None, ROWS),
        P(("yhi", "z"), None, GY, None),
        P(("yhi", "z"), "side", GY, None),
        P(("yhi", "z"), None, GY, None),
        P(("yhi", "z")),
        P(GY, ROWS),
        P(ROWS),
        P(ROWS, GY),
        P(ROWS, GY),
        P(GY, ROWS),
    )
    return jax.shard_map(local, mesh=fine, in_specs=in_specs, out_specs=P(None, None, ROWS), check_vma=False)
```

time: 576 us -> 139 us (0.24)
  waiting for transfers between devices: 292 us -> 0 us
  blocking collectives: 258 us -> 127 us
  between operations: 14.2 us -> 1.08 us
    psum x1 -> x0, waiting for transfers between devices: 292 us -> none  [local(): gate_sum, up_sum = lax.psum((gate_term, up_term), ('side', 'gx'))]
    psum x3 -> x0, blocking collectives: 178 us -> none  [the longest x1 111 us: local(): squares = lax.psum(jnp.sum(middle * middle, axis=1), ('side', 'gx'))]
    all_to_all x0 -> x7, blocking collectives: none -> 127 us  [the longest x5 94.5 us: spread(): lax.all_to_all(jnp.broadcast_to(value, (count, *value.shape)), axes, 0, 0)]
    all_gather x4 -> x0, blocking collectives: 79.6 us -> none  [the longest x1 69.5 us: local(): lax.all_gather(local_rows, 'gx', axis=0, tiled=True)]
  transfers between devices with their start and end apart: 1 -> 0, of which waited for: 1 -> 0; matrix products, arithmetic and copies ran while one was open for 0% -> 0% of each run, Pallas kernels for 0% -> 0%
where the time goes in v1:
time: 139 us; the launch traced here: 138 us
  blocking collectives  127 us (91%)
  matrix products  4.69 us (3%)
  other arithmetic  2.81 us (2%)
  local copies, waits for them, and re-layouts  2.44 us (2%)
    all_to_all x5, blocking collectives, spread(): lax.all_to_all(jnp.broadcast_to(value, (count, *value.shape)), axes, 0, 0)  94.5 us
    all_to_all x1, blocking collectives, local(): over_y = lax.all_to_all(jnp.stack(blocks), Y, 0, 0).astype(f32)  16.4 us
    all_to_all x1, blocking collectives, local(): lax.all_to_all(to_z.reshape(ZS, rows // ZS, -1), 'z', 0, 0).astype(f32)  16.3 us

profile of v1, /device:TPU:1, one launch (start us, length us, event | category | flops | bytes accessed | tf_op | source)
XLA Modules:
  0.0 138.2 jit_solution(13520453130536015214)
XLA Ops:
  0.7 0.7 slice_convert_fusion.2
  1.4 0.8 fusion.55
  2.2 1.3 fusion.54
  3.6 0.2 fusion.26
  3.9 1.2 fusion.4
  5.2 0.2 broadcast_in_dim.55
  5.4 39.1 %all_to_all.35 = bf16[64,2,1152]{2,1,0:T(2,128)(2,1)S(1)} all-to-all(bf16[64,2,1152]{2,1,0:T(2,128)(2,1)S(1)} %broadcast_in_dim.55), channel_id=1, replica_groups=mesh['side'=2,'yhi'=2,'z'=16,'x'=4,'core'=2] {'side','yhi','z'}, dimensions={0} | all-to-all | bytes 589824 | tf_op jit(solution)/shard_map/all_to_all | solution.py:21
  44.5 0.1 reshape.111
  44.8 0.2 mul.114
  45.1 0.8 copy-done.2
  45.9 0.2 convolution_convert_fusion.2
  46.1 12.8 %all_to_all.36 = bf16[8,64,128]{2,1,0:T(8,128)(2,1)S(1)} all-to-all(bf16[8,64,128]{2,1,0:T(8,128)(2,1)S(1)} %broadcast_in_dim.56), channel_id=1, replica_groups=mesh['side'=2,'yhi'=2,'z'=16,'x'=4,'core'=2] {'x','core'}, dimensions={0} | all-to-all | bytes 262144 | tf_op jit(solution)/shard_map/all_to_all | solution.py:21
  59.0 0.1 multiply_reduce_fusion.1
  59.2 0.1 copy.45
  59.4 0.3 convolution_convert_fusion
  59.6 0.3 convolution_convert_fusion.1
  59.9 0.1 fusion.51
  60.1 0.1 pad_maximum_fusion
  60.3 16.4 %all_to_all.37 = bf16[4,64,1920]{2,1,0:T(8,128)(2,1)S(1)} all-to-all(bf16[4,64,1920]{2,1,0:T(8,128)(2,1)S(1)} %pad_maximum_fusion), channel_id=1, replica_groups=mesh['side'=2,'yhi'=2,'z'=16,'x'=4,'core'=2] {'side','yhi'}, dimensions={0} | all-to-all | bytes 1966080 | tf_op jit(solution)/shard_map/all_to_all | solution.py:95
  76.7 0.1 convert_reduce_fusion
  77.2 0.1 copy.48
  77.4 16.3 %all_to_all.38 = bf16[16,4,1920]{2,1,0:T(4,128)(2,1)S(1)} all-to-all(bf16[16,4,1920]{2,1,0:T(4,128)(2,1)S(1)} %reshape.112), channel_id=1, replica_groups=mesh['side'=2,'yhi'=2,'z'=16,'x'=4,'core'=2] {'z'}, dimensions={0} | all-to-all | bytes 491520 | tf_op jit(solution)/shard_map/all_to_all | solution.py:102
  93.7 0.1 convert_reduce_fusion.1
  93.8 0.2 fusion.39
  94.1 20.8 %all_to_all.39 = bf16[16,4,896]{2,1,0:T(4,128)(2,1)S(1)} all-to-all(bf16[16,4,896]{2,1,0:T(4,128)(2,1)S(1)} %broadcast_in_dim.57), channel_id=1, replica_groups=mesh['side'=2,'yhi'=2,'z'=16,'x'=4,'core'=2] {'z'}, dimensions={0} | all-to-all | bytes 229376 | tf_op jit(solution)/shard_map/all_to_all | solution.py:21
  115.0 8.8 %all_to_all.40 = bf16[4,64,896]{2,1,0:T(8,128)(2,1)S(1)} all-to-all(bf16[4,64,896]{2,1,0:T(8,128)(2,1)S(1)} %broadcast_in_dim.58), channel_id=1, replica_groups=mesh['side'=2,'yhi'=2,'z'=16,'x'=4,'core'=2] {'side','yhi'}, dimensions={0} | all-to-all | bytes 917504 | tf_op jit(solution)/shard_map/all_to_all | solution.py:21
  123.8 0.2 fusion.22
  124.0 0.2 convolution_add_fusion.2
  124.1 0.2 convolution_add_fusion.1
  124.3 0.2 fusion.1
  124.5 13.0 %all_to_all.41 = bf16[8,64,128]{2,1,0:T(8,128)(2,1)S(1)} all-to-all(bf16[8,64,128]{2,1,0:T(8,128)(2,1)S(1)} %broadcast_in_dim.59), channel_id=1, replica_groups=mesh['side'=2,'yhi'=2,'z'=16,'x'=4,'core'=2] {'x','core'}, dimensions={0} | all-to-all | bytes 262144 | tf_op jit(solution)/shard_map/all_to_all | solution.py:21
  137.6 0.6 add_convert_fusion
  (52 shorter events, 1.5 us)
Async XLA Ops:
  0.0 59.4 %copy-start = (bf16[128,3584]{1,0:T(8,128)(2,1)S(1)}, bf16[128,3584]{1,0:T(8,128)(2,1)}, u32[]{:S(2)}) copy-start(bf16[128,3584]{1,0:T(8,128)(2,1)} %param.18) | copy-start | bytes 2752516
  45.0 1.0 copy-start.2
  45.1 13.9 %copy-start.4 = (bf16[32,2,128]{2,1,0:T(2,128)(2,1)S(1)}, bf16[32,2,128]{2,1,0:T(2,128)(2,1)}, u32[]{:S(2)}) copy-start(bf16[32,2,128]{2,1,0:T(2,128)(2,1)} %param.10) | copy-start | bytes 49156
  45.1 14.3 %copy-start.5 = (f32[128]{0:T(128)S(1)}, f32[128]{0:T(128)}, u32[]{:S(2)}) copy-start(f32[128]{0:T(128)} %param.16) | copy-start | bytes 1540
  46.1 13.5 %copy-start.1 = (bf16[128,3584]{1,0:T(8,128)(2,1)S(1)}, bf16[128,3584]{1,0:T(8,128)(2,1)}, u32[]{:S(2)}) copy-start(bf16[128,3584]{1,0:T(8,128)(2,1)} %param.17) | copy-start | bytes 2752516
  94.1 29.7 %copy-start.3 = (bf16[3584,128]{1,0:T(8,128)(2,1)S(1)}, bf16[3584,128]{1,0:T(8,128)(2,1)}, u32[]{:S(2)}) copy-start(bf16[3584,128]{1,0:T(8,128)(2,1)} %param.19) | copy-start | bytes 2752516

commit v2 on v1

v2 whole, which is shorter than its diff:
```python
import functools
import math

import jax
import jax.numpy as jnp
from jax import lax
from jax.experimental import pallas as pl
from jax.experimental.pallas import tpu as pltpu
from jax.sharding import Mesh, PartitionSpec as P

D = 8192
EPS = 1e-05
big_negative = -1e30
bf16 = jnp.bfloat16
f32 = jnp.float32

LANES = 128
SIDES, YS, ZQ, ZP = 2, 4, 8, 2
ZS = ZQ * ZP
ROWS = ("side", "yhi", "zq", "zp")
Y = ("side", "yhi")
Z = ("zq", "zp")
NEAR = ("side", "yhi", "zp")
GY = ("x", "core")
GYS = 8


def spread(value, axes, count):
    return lax.all_to_all(jnp.broadcast_to(value, (count, *value.shape)), axes, 0, 0)


SMALL = pltpu.CompilerParams(vmem_limit_bytes=12 * 2**20)


def vmem(count):
    return [pl.BlockSpec(memory_space=pltpu.VMEM)] * count


def split(total):
    high = total.astype(bf16).astype(f32)
    return high, total - high


def attention_kernel(length_ref, query_ref, cache_ref, fresh_ref, out_ref):
    side = lax.axis_index("side")
    half, doubled = cache_ref.shape
    head = doubled // 2
    pairs = query_ref.shape[0]
    group = pairs // 2
    scale = 1.0 / math.sqrt(head)
    contract_last = (((1,), (1,)), ((), ()))
    query = query_ref[...]
    scores = lax.dot_general(query, cache_ref[:, :head], contract_last, preferred_element_type=f32) * scale
    usable = side * half + lax.broadcasted_iota(jnp.int32, (pairs, half), 1) < length_ref[0]
    scores = jnp.where(usable, scores, big_negative)
    fresh = fresh_ref[...].astype(f32)
    draft = lax.broadcasted_iota(jnp.int32, (pairs, 1), 0) // group
    wide = query.astype(f32)
    new_scores, seen = [], []
    for u in range(2):
        seen.append((draft >= u) & (side == SIDES - 1))
        score = jnp.sum(wide * fresh[u : u + 1, :head], axis=1, keepdims=True) * scale
        new_scores.append(jnp.where(seen[u], score, big_negative))
    peak = jnp.max(scores, axis=1, keepdims=True)
    peak = jnp.maximum(peak, jnp.maximum(new_scores[0], new_scores[1]))
    peak = peak.astype(bf16).astype(f32)
    weights = jnp.where(usable, jnp.exp(scores - peak), 0.0)
    total = jnp.sum(weights, axis=1, keepdims=True)
    accum = jnp.dot(weights.astype(bf16), cache_ref[:, head:], preferred_element_type=f32)
    for u in range(2):
        weight = jnp.where(seen[u], jnp.exp(new_scores[u] - peak), 0.0)
        total = total + weight
        accum = accum + weight.astype(bf16).astype(f32) * fresh[u : u + 1, head:]
    mixed = accum / total
    high, low = split(total)
    lane = lax.broadcasted_iota(jnp.int32, (pairs, LANES), 1)
    row = lax.broadcasted_iota(jnp.int32, (pairs, LANES), 0) % group
    stats = jnp.where(lane == row, peak, 0.0)
    stats = jnp.where(lane == row + group, high, stats)
    stats = jnp.where(lane == row + 2 * group, low, stats)
    stats = [jnp.sum(stats[t * group : (t + 1) * group], axis=0, keepdims=True) for t in range(2)]
    for i in range(group):
        both = jnp.concatenate([mixed[i : i + 1], mixed[group + i : group + i + 1]], axis=0)
        out_ref[:, i * head : (i + 1) * head] = both.astype(bf16)
    out_ref[:, group * head :] = jnp.concatenate(stats, axis=0).astype(bf16)


def project_kernel(group, parts_ref, weight_ref, out_ref):
    width = weight_ref.shape[0]
    head = width // group
    stats = [parts_ref[s, :, width:].astype(f32) for s in range(SIDES)]
    totals = [stat[:, group : 2 * group] + stat[:, 2 * group : 3 * group] for stat in stats]
    peaks = [stat[:, :group] for stat in stats]
    peak = jnp.maximum(peaks[0], peaks[1])
    shares = [totals[s] * jnp.exp(peaks[s] - peak) for s in range(SIDES)]
    whole = shares[0] + shares[1]
    shares = [share / whole for share in shares]
    merged = []
    for i in range(group):
        columns = slice(i * head, (i + 1) * head)
        value = parts_ref[0, :, columns].astype(f32) * shares[0][:, i : i + 1]
        value = value + parts_ref[1, :, columns].astype(f32) * shares[1][:, i : i + 1]
        merged.append(value.astype(bf16))
    total = jnp.dot(jnp.concatenate(merged, axis=1), weight_ref[...], preferred_element_type=f32).astype(bf16)
    for k in range(out_ref.shape[0]):
        out_ref[k] = total


def gate_kernel(parts_ref, hidden_ref, gain_ref, gate_ref, up_ref, middle_ref, out_ref):
    middle = hidden_ref[...].astype(f32)
    for k in range(parts_ref.shape[0]):
        middle = middle + parts_ref[k].astype(f32)
    middle_ref[...] = middle
    rows = middle.shape[0]
    step = rows // ZS
    high, low = split(jnp.sum(middle * middle, axis=1, keepdims=True))
    lane = lax.broadcasted_iota(jnp.int32, (rows, LANES), 1)
    stats = jnp.where(lane == 0, high, jnp.where(lane == 1, low, 0.0))
    scaled = middle * gain_ref[...]

    def regroup(value):
        pieces = [value[(q * ZP + p) * step : (q * ZP + p + 1) * step] for p in range(ZP) for q in range(ZQ)]
        return jnp.concatenate(pieces, axis=0).astype(bf16)

    scaled, stats = regroup(scaled), regroup(stats)
    part = gate_ref.shape[1] // YS
    half = rows // ZP
    for y in range(YS):
        columns = slice(y * part, (y + 1) * part)
        for start, ref in ((0, gate_ref), (part, up_ref)):
            term = jnp.dot(scaled, ref[:, columns], preferred_element_type=f32).astype(bf16)
            for p in range(ZP):
                out_ref[y * ZP + p, :, start : start + part] = term[p * half : (p + 1) * half]
        for p in range(ZP):
            out_ref[y * ZP + p, :, 2 * part :] = stats[p * half : (p + 1) * half]


def sum_kernel(parts_ref, out_ref):
    total = parts_ref[0].astype(f32)
    for k in range(1, parts_ref.shape[0]):
        total = total + parts_ref[k].astype(f32)
    width = total.shape[1] - LANES
    stats = total[:, width:]
    high, low = split(stats[:, :1] + stats[:, 1:2])
    lane = lax.broadcasted_iota(jnp.int32, stats.shape, 1)
    stats = jnp.where(lane == 0, high, jnp.where(lane == 1, low, 0.0)).astype(bf16)
    total = total[:, :width].astype(bf16)
    step = out_ref.shape[1]
    for q in range(out_ref.shape[0]):
        out_ref[q, :, :width] = total[q * step : (q + 1) * step]
        out_ref[q, :, width:] = stats[q * step : (q + 1) * step]


def activate_kernel(parts_ref, out_ref):
    total = parts_ref[0].astype(f32)
    for k in range(1, parts_ref.shape[0]):
        total = total + parts_ref[k].astype(f32)
    part = out_ref.shape[2]
    squares = total[:, 2 * part : 2 * part + 1] + total[:, 2 * part + 1 : 2 * part + 2]
    factor = lax.rsqrt(squares / D + EPS)
    gate = total[:, :part] * factor
    up = total[:, part : 2 * part] * factor
    activated = (gate / (1.0 + jnp.exp(-gate)) * up).astype(bf16)
    for k in range(out_ref.shape[0]):
        out_ref[k] = activated


def down_kernel(active_ref, weight_ref, out_ref):
    part = active_ref.shape[2]
    total = jnp.dot(active_ref[0], weight_ref[:part], preferred_element_type=f32)
    for y in range(1, YS):
        total = total + jnp.dot(active_ref[y], weight_ref[y * part : (y + 1) * part], preferred_element_type=f32)
    total = total.astype(bf16)
    for k in range(out_ref.shape[0]):
        out_ref[k] = total


def local(hidden_in, queries, kv_cache, new_kv, lengths, out_weight, norm_gain, gate_weight, up_weight, down_weight):
    group, head = queries.shape[2:]
    rows = hidden_in.shape[0] * 2
    cols = hidden_in.shape[2]
    width = out_weight.shape[0]
    part = gate_weight.shape[1] // YS
    step = rows // ZS
    shape = jax.ShapeDtypeStruct
    hidden = hidden_in.reshape(rows, cols)

    own = pl.pallas_call(
        attention_kernel,
        out_shape=shape((2, width + LANES), bf16),
        in_specs=[pl.BlockSpec(memory_space=pltpu.SMEM)] + vmem(3),
        out_specs=vmem(1)[0],
        name="attention",
        compiler_params=SMALL,
    )(lengths, queries.reshape(2 * group, head), kv_cache.reshape(-1, 2 * head), new_kv.reshape(2, 2 * head))
    everyone = spread(own, ROWS, YS * ZS).reshape(SIDES, rows, width + LANES)
    head_parts = pl.pallas_call(
        functools.partial(project_kernel, group),
        out_shape=shape((GYS, rows, cols), bf16),
        in_specs=vmem(2),
        out_specs=vmem(1)[0],
        name="project",
        compiler_params=SMALL,
    )(everyone, out_weight)
    head_parts = lax.all_to_all(head_parts, GY, 0, 0)
    middle, terms = pl.pallas_call(
        gate_kernel,
        out_shape=[shape((rows, cols), f32), shape((YS * ZP, rows // ZP, 2 * part + LANES), bf16)],
        in_specs=vmem(5),
        out_specs=vmem(2),
        name="gate_up",
        compiler_params=SMALL,
    )(head_parts, hidden, norm_gain.reshape(1, cols), gate_weight, up_weight)
    terms = lax.all_to_all(terms, NEAR, 0, 0)
    terms = pl.pallas_call(
        sum_kernel,
        out_shape=shape((ZQ, step, 2 * part + LANES), bf16),
        in_specs=vmem(1),
        out_specs=vmem(1)[0],
        name="near_sum",
        compiler_params=SMALL,
    )(terms)
    terms = lax.all_to_all(terms, "zq", 0, 0)
    activated = pl.pallas_call(
        activate_kernel,
        out_shape=shape((ZS, step, part), bf16),
        in_specs=vmem(1),
        out_specs=vmem(1)[0],
        name="activate",
        compiler_params=SMALL,
    )(terms)
    along_z = lax.all_to_all(activated, Z, 0, 0).reshape(rows, part)
    along_y = spread(along_z, Y, YS)
    ffn_parts = pl.pallas_call(
        down_kernel,
        out_shape=shape((GYS, rows, cols), bf16),
        in_specs=vmem(2),
        out_specs=vmem(1)[0],
        name="down",
        compiler_params=SMALL,
    )(along_y, down_weight)
    ffn_sum = jnp.sum(lax.all_to_all(ffn_parts, GY, 0, 0).astype(f32), axis=0)
    return (middle + ffn_sum).astype(bf16).reshape(hidden_in.shape)


def solution(mesh):
    fine = Mesh(mesh.devices.reshape(2, 2, ZQ, ZP, 4, 2), ("side", "yhi", "zq", "zp", "x", "core"))
    requests = ("yhi", "zq", "zp")
    in_specs = (
        P(None, None, ROWS),
        P(requests, None, GY, None),
        P(requests, "side", GY, None),
        P(requests, None, GY, None),
        P(requests),
        P(GY, ROWS),
        P(ROWS),
        P(ROWS, GY),
        P(ROWS, GY),
        P(GY, ROWS),
    )
    return jax.shard_map(local, mesh=fine, in_specs=in_specs, out_specs=P(None, None, ROWS), check_vma=False)
```

time: 139 us -> 131 us (0.942)
  matrix products: 4.69 us -> 0 us
  blocking collectives: 127 us -> 124 us
  other arithmetic: 2.81 us -> 0.63 us
  Pallas kernels: 0 us -> 2.01 us
    all_to_all x5 -> x2, blocking collectives: 94.5 us -> 48.2 us  [spread(): lax.all_to_all(jnp.broadcast_to(value, (count, *value.shape)), axes, 0, 0)]
    all_to_all x2 -> x5, blocking collectives: 32.7 us -> 75.9 us  [the longest x1 17.7 us: local(): terms = lax.all_to_all(terms, NEAR, 0, 0)]
    dot_general x10 -> x0, matrix products: 4.69 us -> none  [the longest x1 1.25 us: partial_attention(): lax.dot_general(query, cache[:, :head], contract_last, preferred_element_...]
    pallas_call x0 -> x6, Pallas kernels: none -> 2.01 us  [the longest x1 0.45 us: local(): pl.pallas_call(functools.partial(project_kernel, group), out_shape=shape(...]
    unnamed x14 -> x18, local copies, waits for them, and re-layouts: 0.94 us -> 2.38 us
where the time goes in v2:
time: 131 us; the launch traced here: 130 us
  blocking collectives  124 us (95%)
  local copies, waits for them, and re-layouts  2.72 us (2%)
  Pallas kernels  2.01 us (2%)
    all_to_all x2, blocking collectives, spread(): lax.all_to_all(jnp.broadcast_to(value, (count, *value.shape)), axes, 0, 0)  48.2 us
    all_to_all x1, blocking collectives, local(): terms = lax.all_to_all(terms, NEAR, 0, 0)  17.7 us
    all_to_all x1, blocking collectives, local(): terms = lax.all_to_all(terms, 'zq', 0, 0)  16.6 us
    all_to_all x1, blocking collectives, local(): along_z = lax.all_to_all(activated, Z, 0, 0).reshape(rows, part)  14.5 us
    all_to_all x1, blocking collectives, local(): ffn_sum = jnp.sum(lax.all_to_all(ffn_parts, GY, 0, 0).astype(f32), axis=0)  14.2 us
    all_to_all x1, blocking collectives, local(): head_parts = lax.all_to_all(head_parts, GY, 0, 0)  12.8 us

profile of v2, /device:TPU:1, one launch (start us, length us, event | category | flops | bytes accessed | tf_op | source)
XLA Modules:
  0.0 130.2 jit_solution(6590071223797874257)
XLA Ops:
  0.0 0.0 copy-start.6
  0.7 0.0 copy-start.7
  0.7 0.0 copy-done.6
  0.7 0.7 copy-done.7
  1.3 0.0 copy-start.3
  1.4 1.0 copy-done.3
  2.4 0.4 attention.1
  2.8 0.2 broadcast_in_dim.6
  3.0 0.0 copy-start.4
  3.0 0.0 copy-start.1
  3.0 39.2 %all_to_all.35 = bf16[64,2,1152]{2,1,0:T(2,128)(2,1)S(1)} all-to-all(bf16[64,2,1152]{2,1,0:T(2,128)(2,1)S(1)} %broadcast_in_dim.6), channel_id=1, replica_groups=mesh['side'=2,'yhi'=2,'zq'=8,'zp'=2,'x'=4,'core'=2] {'side','yhi','zq','..., dimensions={0} | all-to-all | bytes 589824 | tf_op jit(solution)/shard_map/all_to_all | solution.py:29
  42.2 0.0 copy-start
  42.2 0.1 reshape.27.parts_ref
  42.4 0.0 copy-done.4
  42.4 0.4 project.1
  42.8 0.0 copy-start.5
  42.8 12.8 %all_to_all.36.parts_ref = bf16[8,64,128]{2,1,0:T(8,128)(2,1)S(1)} all-to-all(bf16[8,64,128]{2,1,0:T(8,128)(2,1)S(1)} %project.1), channel_id=1, replica_groups=mesh['side'=2,'yhi'=2,'zq'=8,'zp'=2,'x'=4,'core'=2] {'x','core'}, dimensions={0} | all-to-all | bytes 262144 | tf_op jit(solution)/shard_map/all_to_all | solution.py:205
  55.6 0.0 copy-done.1
  55.6 0.0 copy-done
  55.6 0.0 copy-done.5
  55.6 0.6 copy-done.8
  56.3 0.4 gate_up.1
  56.7 17.7 %all_to_all.37.parts_ref = bf16[8,32,1920]{2,1,0:T(8,128)(2,1)S(1)} all-to-all(bf16[8,32,1920]{2,1,0:T(8,128)(2,1)S(1)} %get-tuple-element.8), channel_id=1, replica_groups=mesh['side'=2,'yhi'=2,'zq'=8,'zp'=2,'x'=4,'core'=2] {'side','yhi','zp'}, dimensions={0} | all-to-all | bytes 1966080 | tf_op jit(solution)/shard_map/all_to_all | solution.py:214
  74.4 0.2 near_sum.1
  74.7 16.6 %all_to_all.38.parts_ref = bf16[8,4,1920]{2,1,0:T(4,128)(2,1)S(1)} all-to-all(bf16[8,4,1920]{2,1,0:T(4,128)(2,1)S(1)} %near_sum.1), channel_id=1, replica_groups=mesh['side'=2,'yhi'=2,'zq'=8,'zp'=2,'x'=4,'core'=2] {'zq'}, dimensions={0} | all-to-all | bytes 245760 | tf_op jit(solution)/shard_map/all_to_all | solution.py:223
  91.3 0.2 activate.1
  91.5 14.5 %all_to_all.39 = bf16[16,4,896]{2,1,0:T(4,128)(2,1)S(1)} all-to-all(bf16[16,4,896]{2,1,0:T(4,128)(2,1)S(1)} %activate.1), channel_id=1, replica_groups=mesh['side'=2,'yhi'=2,'zq'=8,'zp'=2,'x'=4,'core'=2] {'zq','zp'}, dimensions={0} | all-to-all | bytes 229376 | tf_op jit(solution)/shard_map/all_to_all | solution.py:232
  106.0 8.9 %all_to_all.40.active_ref = bf16[4,64,896]{2,1,0:T(8,128)(2,1)S(1)} all-to-all(bf16[4,64,896]{2,1,0:T(8,128)(2,1)S(1)} %broadcast_in_dim.7), channel_id=1, replica_groups=mesh['side'=2,'yhi'=2,'zq'=8,'zp'=2,'x'=4,'core'=2] {'side','yhi'}, dimensions={0} | all-to-all | bytes 917504 | tf_op jit(solution)/shard_map/all_to_all | solution.py:29
  115.0 0.0 copy-done.2
  115.0 0.3 down.1
  115.3 14.2 %all_to_all.41 = bf16[8,64,128]{2,1,0:T(8,128)(2,1)S(1)} all-to-all(bf16[8,64,128]{2,1,0:T(8,128)(2,1)S(1)} %down.1), channel_id=1, replica_groups=mesh['side'=2,'yhi'=2,'zq'=8,'zp'=2,'x'=4,'core'=2] {'x','core'}, dimensions={0} | all-to-all | bytes 262144 | tf_op jit(solution)/shard_map/all_to_all | solution.py:242
  129.5 0.6 add_convert_fusion
  (5 shorter events, 0.1 us)
Async XLA Ops:
  0.0 0.7 copy-start.6
  0.7 0.7 copy-start.7
  1.3 1.0 copy-start.3
  3.0 39.4 %copy-start.4 = (bf16[1024,128]{1,0:T(8,128)(2,1)S(1)}, bf16[1024,128]{1,0:T(8,128)(2,1)}, u32[]{:S(2)}) copy-start(bf16[1024,128]{1,0:T(8,128)(2,1)} %weight_ref.2) | copy-start | bytes 786436
  3.0 52.6 %copy-start.1 = (bf16[128,3584]{1,0:T(8,128)(2,1)S(1)}, bf16[128,3584]{1,0:T(8,128)(2,1)}, u32[]{:S(2)}) copy-start(bf16[128,3584]{1,0:T(8,128)(2,1)} %up_ref.1) | copy-start | bytes 2752516
  42.2 13.4 %copy-start = (bf16[128,3584]{1,0:T(8,128)(2,1)S(1)}, bf16[128,3584]{1,0:T(8,128)(2,1)}, u32[]{:S(2)}) copy-start(bf16[128,3584]{1,0:T(8,128)(2,1)} %gate_ref.1) | copy-start | bytes 2752516
  42.8 12.8 %copy-start.5 = (bf16[32,2,128]{2,1,0:T(2,128)(2,1)S(1)}, bf16[32,2,128]{2,1,0:T(2,128)(2,1)}, u32[]{:S(2)}) copy-start(bf16[32,2,128]{2,1,0:T(2,128)(2,1)} %param.10) | copy-start | bytes 49156
  55.6 0.7 copy-start.8
  106.0 9.0 %copy-start.2 = (bf16[3584,128]{1,0:T(8,128)(2,1)S(1)}, bf16[3584,128]{1,0:T(8,128)(2,1)}, u32[]{:S(2)}) copy-start(bf16[3584,128]{1,0:T(8,128)(2,1)} %weight_ref.3) | copy-start | bytes 2752516

commit v3 on v2

--- a/solution.py
+++ b/solution.py
@@ -41,7 +41,33 @@
     return high, total - high
 
 
-def attention_kernel(length_ref, query_ref, cache_ref, fresh_ref, out_ref):
+def attention_kernel(
+    length_ref,
+    query_hbm,
+    cache_hbm,
+    fresh_hbm,
+    hidden_hbm,
+    gain_hbm,
+    out_ref,
+    hidden_ref,
+    gain_ref,
+    query_ref,
+    cache_ref,
+    fresh_ref,
+    arrived,
+):
+    moves = (
+        (cache_hbm, cache_ref),
+        (query_hbm, query_ref),
+        (fresh_hbm, fresh_ref),
+        (hidden_hbm, hidden_ref),
+        (gain_hbm, gain_ref),
+    )
+    copies = [pltpu.make_async_copy(source, target, arrived.at[k]) for k, (source, target) in enumerate(moves)]
+    for copy in copies:
+        copy.start()
+    for copy in copies:
+        copy.wait()
     side = lax.axis_index("side")
     half, doubled = cache_ref.shape
     head = doubled // 2
@@ -183,17 +209,35 @@
     part = gate_weight.shape[1] // YS
     step = rows // ZS
     shape = jax.ShapeDtypeStruct
-    hidden = hidden_in.reshape(rows, cols)
-
-    own = pl.pallas_call(
+
+    own, hidden, gain = pl.pallas_call(
         attention_kernel,
-        out_shape=shape((2, width + LANES), bf16),
-        in_specs=[pl.BlockSpec(memory_space=pltpu.SMEM)] + vmem(3),
-        out_specs=vmem(1)[0],
+        out_shape=[shape((2, width + LANES), bf16), shape((rows, cols), bf16), shape((1, cols), f32)],
+        in_specs=[pl.BlockSpec(memory_space=pltpu.SMEM)] + [pl.BlockSpec(memory_space=pltpu.HBM)] * 5,
+        out_specs=vmem(3),
+        scratch_shapes=[
+            pltpu.VMEM((2 * group, head), bf16),
+            pltpu.VMEM((kv_cache.shape[1], 2 * head), bf16),
+            pltpu.VMEM((2, 2 * head), bf16),
+            pltpu.SemaphoreType.DMA((5,)),
+        ],
         name="attention",
         compiler_params=SMALL,
-    )(lengths, queries.reshape(2 * group, head), kv_cache.reshape(-1, 2 * head), new_kv.reshape(2, 2 * head))
-    everyone = spread(own, ROWS, YS * ZS).reshape(SIDES, rows, width + LANES)
+    )(
+        lengths,
+        *(
+            pltpu.with_memory_space_constraint(value, pltpu.HBM)
+            for value in (
+                queries.reshape(2 * group, head),
+                kv_cache.reshape(-1, 2 * head),
+                new_kv.reshape(2, 2 * head),
+                hidden_in.reshape(rows, cols),
+                norm_gain.reshape(1, cols),
+            )
+        ),
+    )
+    along_z = spread(own, Z, ZS).reshape(2 * ZS, width + LANES)
+    everyone = spread(along_z, Y, YS).reshape(SIDES, rows, width + LANES)
     head_parts = pl.pallas_call(
         functools.partial(project_kernel, group),
         out_shape=shape((GYS, rows, cols), bf16),
@@ -210,7 +254,7 @@
         out_specs=vmem(2),
         name="gate_up",
         compiler_params=SMALL,
-    )(head_parts, hidden, norm_gain.reshape(1, cols), gate_weight, up_weight)
+    )(head_parts, hidden, gain, gate_weight, up_weight)
     terms = lax.all_to_all(terms, NEAR, 0, 0)
     terms = pl.pallas_call(
         sum_kernel,

time: 131 us -> 125 us (0.954)
  blocking collectives: 124 us -> 120 us
  local copies, waits for them, and re-layouts: 2.72 us -> 0.19 us
    unnamed x18 -> x8, local copies, waits for them, and re-layouts: 2.38 us -> 0.02 us
    all_to_all x2 -> x3, blocking collectives: 48.2 us -> 46 us  [spread(): lax.all_to_all(jnp.broadcast_to(value, (count, *value.shape)), axes, 0, 0)]
    all_to_all x1, blocking collectives: 17.7 us -> 16.1 us  [local(): terms = lax.all_to_all(terms, NEAR, 0, 0)]
where the time goes in v3:
time: 125 us
  blocking collectives  120 us (96%)
  Pallas kernels  3.12 us (2%)
    all_to_all x3, blocking collectives, spread(): lax.all_to_all(jnp.broadcast_to(value, (count, *value.shape)), axes, 0, 0)  46 us
    all_to_all x1, blocking collectives, local(): terms = lax.all_to_all(terms, 'zq', 0, 0)  16.2 us
    all_to_all x1, blocking collectives, local(): terms = lax.all_to_all(terms, NEAR, 0, 0)  16.1 us
    all_to_all x1, blocking collectives, local(): along_z = lax.all_to_all(activated, Z, 0, 0).reshape(rows, part)  14.7 us
    all_to_all x1, blocking collectives, local(): ffn_sum = jnp.sum(lax.all_to_all(ffn_parts, GY, 0, 0).astype(f32), axis=0)  13.9 us
    all_to_all x1, blocking collectives, local(): head_parts = lax.all_to_all(head_parts, GY, 0, 0)  13.1 us

profile of v3, /device:TPU:1, one launch (start us, length us, event | category | flops | bytes accessed | tf_op | source)
XLA Modules:
  0.0 124.8 jit_solution(7695886327560207521)
XLA Ops:
  0.7 1.5 %attention.1 = (bf16[2,1152]{1,0:T(2,128)(2,1)S(1)}, bf16[64,128]{1,0:T(8,128)(2,1)S(1)}, f32[1,128]{1,0:T(1,128)S(1)}) custom-call(s32[1]{0:T(128)S(6)} %copy.11.length_ref, bf16[16,128]{1,0:T(8,128)(2,1)} %bitcast.10, bf16[1024,256]{1,0:T(8,128)(2,1)} %bitcast.8, bf16[2,256]{1,0:T(2,128)(2,1)} %bitcast.11, bf16[64,128]{1,0:T(8,128)(2,1)} %bitcast.9, ...), custom_call_target="tpu_custom_call" | custom-call | tf_op jit(solution)/shard_map/attention/pallas_call | solution.py:213
  2.2 0.0 copy-start.3
  2.2 27.4 %all_to_all.40 = bf16[16,2,1152]{2,1,0:T(2,128)(2,1)S(1)} all-to-all(bf16[16,2,1152]{2,1,0:T(2,128)(2,1)S(1)} %broadcast_in_dim.9), channel_id=1, replica_groups=mesh['side'=2,'yhi'=2,'zq'=8,'zp'=2,'x'=4,'core'=2] {'zq','zp'}, dimensions={0} | all-to-all | bytes 147456 | tf_op jit(solution)/shard_map/all_to_all | solution.py:29
  29.6 0.0 copy-start
  29.7 0.0 copy-start.1
  29.7 9.7 %all_to_all.41 = bf16[4,32,1152]{2,1,0:T(8,128)(2,1)S(1)} all-to-all(bf16[4,32,1152]{2,1,0:T(8,128)(2,1)S(1)} %broadcast_in_dim.10), channel_id=1, replica_groups=mesh['side'=2,'yhi'=2,'zq'=8,'zp'=2,'x'=4,'core'=2] {'side','yhi'}, dimensions={0} | all-to-all | bytes 589824 | tf_op jit(solution)/shard_map/all_to_all | solution.py:29
  39.4 0.0 copy-done.3
  39.4 0.4 project.1
  39.9 13.1 %all_to_all.42.parts_ref = bf16[8,64,128]{2,1,0:T(8,128)(2,1)S(1)} all-to-all(bf16[8,64,128]{2,1,0:T(8,128)(2,1)S(1)} %project.1), channel_id=1, replica_groups=mesh['side'=2,'yhi'=2,'zq'=8,'zp'=2,'x'=4,'core'=2] {'x','core'}, dimensions={0} | all-to-all | bytes 262144 | tf_op jit(solution)/shard_map/all_to_all | solution.py:249
  53.0 0.0 copy-done
  53.0 0.0 copy-done.1
  53.0 0.4 gate_up.1
  53.4 16.1 %all_to_all.43.parts_ref = bf16[8,32,1920]{2,1,0:T(8,128)(2,1)S(1)} all-to-all(bf16[8,32,1920]{2,1,0:T(8,128)(2,1)S(1)} %get-tuple-element.14), channel_id=1, replica_groups=mesh['side'=2,'yhi'=2,'zq'=8,'zp'=2,'x'=4,'core'=2] {'side','yhi','zp'}, dimensions={0} | all-to-all | bytes 1966080 | tf_op jit(solution)/shard_map/all_to_all | solution.py:258
  69.5 0.2 near_sum.1
  69.8 16.2 %all_to_all.44.parts_ref = bf16[8,4,1920]{2,1,0:T(4,128)(2,1)S(1)} all-to-all(bf16[8,4,1920]{2,1,0:T(4,128)(2,1)S(1)} %near_sum.1), channel_id=1, replica_groups=mesh['side'=2,'yhi'=2,'zq'=8,'zp'=2,'x'=4,'core'=2] {'zq'}, dimensions={0} | all-to-all | bytes 245760 | tf_op jit(solution)/shard_map/all_to_all | solution.py:267
  86.0 0.2 activate.1
  86.2 14.7 %all_to_all.45 = bf16[16,4,896]{2,1,0:T(4,128)(2,1)S(1)} all-to-all(bf16[16,4,896]{2,1,0:T(4,128)(2,1)S(1)} %activate.1), channel_id=1, replica_groups=mesh['side'=2,'yhi'=2,'zq'=8,'zp'=2,'x'=4,'core'=2] {'zq','zp'}, dimensions={0} | all-to-all | bytes 229376 | tf_op jit(solution)/shard_map/all_to_all | solution.py:276
  100.9 0.0 copy-start.2
  101.0 8.9 %all_to_all.46.active_ref = bf16[4,64,896]{2,1,0:T(8,128)(2,1)S(1)} all-to-all(bf16[4,64,896]{2,1,0:T(8,128)(2,1)S(1)} %broadcast_in_dim.11), channel_id=1, replica_groups=mesh['side'=2,'yhi'=2,'zq'=8,'zp'=2,'x'=4,'core'=2] {'side','yhi'}, dimensions={0} | all-to-all | bytes 917504 | tf_op jit(solution)/shard_map/all_to_all | solution.py:29
  109.9 0.0 copy-done.2
  109.9 0.3 down.1
  110.2 13.9 %all_to_all.47 = bf16[8,64,128]{2,1,0:T(8,128)(2,1)S(1)} all-to-all(bf16[8,64,128]{2,1,0:T(8,128)(2,1)S(1)} %down.1), channel_id=1, replica_groups=mesh['side'=2,'yhi'=2,'zq'=8,'zp'=2,'x'=4,'core'=2] {'x','core'}, dimensions={0} | all-to-all | bytes 262144 | tf_op jit(solution)/shard_map/all_to_all | solution.py:286
  124.2 0.6 add_convert_fusion
  (6 shorter events, 0.2 us)
Async XLA Ops:
  2.2 37.2 %copy-start.3 = (bf16[1024,128]{1,0:T(8,128)(2,1)S(1)}, bf16[1024,128]{1,0:T(8,128)(2,1)}, u32[]{:S(2)}) copy-start(bf16[1024,128]{1,0:T(8,128)(2,1)} %weight_ref.2) | copy-start | bytes 786436
  29.6 23.4 %copy-start = (bf16[128,3584]{1,0:T(8,128)(2,1)S(1)}, bf16[128,3584]{1,0:T(8,128)(2,1)}, u32[]{:S(2)}) copy-start(bf16[128,3584]{1,0:T(8,128)(2,1)} %gate_ref.1) | copy-start | bytes 2752516
  29.7 23.4 %copy-start.1 = (bf16[128,3584]{1,0:T(8,128)(2,1)S(1)}, bf16[128,3584]{1,0:T(8,128)(2,1)}, u32[]{:S(2)}) copy-start(bf16[128,3584]{1,0:T(8,128)(2,1)} %up_ref.1) | copy-start | bytes 2752516
  100.9 9.0 %copy-start.2 = (bf16[3584,128]{1,0:T(8,128)(2,1)S(1)}, bf16[3584,128]{1,0:T(8,128)(2,1)}, u32[]{:S(2)}) copy-start(bf16[3584,128]{1,0:T(8,128)(2,1)} %weight_ref.3) | copy-start | bytes 2752516

commit v4 on v3

--- a/solution.py
+++ b/solution.py
@@ -14,7 +14,7 @@
 bf16 = jnp.bfloat16
 f32 = jnp.float32
 
-LANES = 128
+LANES, TALL = 128, 8
 SIDES, YS, ZQ, ZP = 2, 4, 8, 2
 ZS = ZQ * ZP
 ROWS = ("side", "yhi", "zq", "zp")
@@ -140,41 +140,52 @@
     rows = middle.shape[0]
     step = rows // ZS
     high, low = split(jnp.sum(middle * middle, axis=1, keepdims=True))
-    lane = lax.broadcasted_iota(jnp.int32, (rows, LANES), 1)
-    stats = jnp.where(lane == 0, high, jnp.where(lane == 1, low, 0.0))
     scaled = middle * gain_ref[...]
 
     def regroup(value):
         pieces = [value[(q * ZP + p) * step : (q * ZP + p + 1) * step] for p in range(ZP) for q in range(ZQ)]
-        return jnp.concatenate(pieces, axis=0).astype(bf16)
-
-    scaled, stats = regroup(scaled), regroup(stats)
+        return jnp.concatenate(pieces, axis=0)
+
+    scaled, high, low = regroup(scaled).astype(bf16), regroup(high), regroup(low)
     part = gate_ref.shape[1] // YS
-    half = rows // ZP
+    tall = out_ref.shape[1]
+    count = rows // ZP // tall
+    lane = lax.broadcasted_iota(jnp.int32, (tall, LANES), 1)
+    for p in range(ZP):
+        stats = jnp.zeros((tall, LANES), f32)
+        for g in range(count):
+            block = slice((p * count + g) * tall, (p * count + g + 1) * tall)
+            stats = jnp.where(lane == 2 * g, high[block], jnp.where(lane == 2 * g + 1, low[block], stats))
+        for y in range(YS):
+            out_ref[y * ZP + p, :, 2 * part * count :] = stats.astype(bf16)
     for y in range(YS):
         columns = slice(y * part, (y + 1) * part)
         for start, ref in ((0, gate_ref), (part, up_ref)):
-            term = jnp.dot(scaled, ref[:, columns], preferred_element_type=f32).astype(bf16)
+            term = jnp.dot(scaled, ref[:, columns], preferred_element_type=f32)
             for p in range(ZP):
-                out_ref[y * ZP + p, :, start : start + part] = term[p * half : (p + 1) * half]
-        for p in range(ZP):
-            out_ref[y * ZP + p, :, 2 * part :] = stats[p * half : (p + 1) * half]
+                for g in range(count):
+                    block = term[(p * count + g) * tall : (p * count + g + 1) * tall].astype(bf16)
+                    out_ref[y * ZP + p, :, 2 * part * g + start : 2 * part * g + start + part] = block
 
 
 def sum_kernel(parts_ref, out_ref):
     total = parts_ref[0].astype(f32)
     for k in range(1, parts_ref.shape[0]):
         total = total + parts_ref[k].astype(f32)
-    width = total.shape[1] - LANES
-    stats = total[:, width:]
-    high, low = split(stats[:, :1] + stats[:, 1:2])
-    lane = lax.broadcasted_iota(jnp.int32, stats.shape, 1)
-    stats = jnp.where(lane == 0, high, jnp.where(lane == 1, low, 0.0)).astype(bf16)
-    total = total[:, :width].astype(bf16)
     step = out_ref.shape[1]
-    for q in range(out_ref.shape[0]):
-        out_ref[q, :, :width] = total[q * step : (q + 1) * step]
-        out_ref[q, :, width:] = stats[q * step : (q + 1) * step]
+    width = out_ref.shape[2] - LANES
+    tall = total.shape[0]
+    each = tall // step
+    count = out_ref.shape[0] // each
+    lane = lax.broadcasted_iota(jnp.int32, (tall, LANES), 1)
+    pairs = total[:, width * count :]
+    for g in range(count):
+        high, low = split(pairs[:, 2 * g : 2 * g + 1] + pairs[:, 2 * g + 1 : 2 * g + 2])
+        stats = jnp.where(lane == 0, high, jnp.where(lane == 1, low, 0.0))
+        for e in range(each):
+            rows = slice(e * step, (e + 1) * step)
+            out_ref[g * each + e, :, :width] = total[rows, g * width : (g + 1) * width].astype(bf16)
+            out_ref[g * each + e, :, width:] = stats[rows].astype(bf16)
 
 
 def activate_kernel(parts_ref, out_ref):
@@ -249,7 +260,7 @@
     head_parts = lax.all_to_all(head_parts, GY, 0, 0)
     middle, terms = pl.pallas_call(
         gate_kernel,
-        out_shape=[shape((rows, cols), f32), shape((YS * ZP, rows // ZP, 2 * part + LANES), bf16)],
+        out_shape=[shape((rows, cols), f32), shape((YS * ZP, TALL, 2 * part * (rows // ZP // TALL) + LANES), bf16)],
         in_specs=vmem(5),
         out_specs=vmem(2),
         name="gate_up",

time: 125 us -> 124 us (level)
  no operation moved by 1% of the time
where the time goes in v4:
time: 124 us
  blocking collectives  119 us (96%)
  Pallas kernels  3.15 us (3%)
    all_to_all x3, blocking collectives, spread(): lax.all_to_all(jnp.broadcast_to(value, (count, *value.shape)), axes, 0, 0)  46 us
    all_to_all x1, blocking collectives, local(): terms = lax.all_to_all(terms, 'zq', 0, 0)  16.2 us
    all_to_all x1, blocking collectives, local(): terms = lax.all_to_all(terms, NEAR, 0, 0)  15.6 us
    all_to_all x1, blocking collectives, local(): along_z = lax.all_to_all(activated, Z, 0, 0).reshape(rows, part)  14.5 us
    all_to_all x1, blocking collectives, local(): ffn_sum = jnp.sum(lax.all_to_all(ffn_parts, GY, 0, 0).astype(f32), axis=0)  13.9 us
    all_to_all x1, blocking collectives, local(): head_parts = lax.all_to_all(head_parts, GY, 0, 0)  13.1 us

profile of v4, /device:TPU:1, one launch (start us, length us, event | category | flops | bytes accessed | tf_op | source)
XLA Modules:
  0.0 124.0 jit_solution(10284253662268287653)
XLA Ops:
  0.7 1.5 %attention.1 = (bf16[2,1152]{1,0:T(2,128)(2,1)S(1)}, bf16[64,128]{1,0:T(8,128)(2,1)S(1)}, f32[1,128]{1,0:T(1,128)S(1)}) custom-call(s32[1]{0:T(128)S(6)} %copy.11.length_ref, bf16[16,128]{1,0:T(8,128)(2,1)} %bitcast.10, bf16[1024,256]{1,0:T(8,128)(2,1)} %bitcast.8, bf16[2,256]{1,0:T(2,128)(2,1)} %bitcast.11, bf16[64,128]{1,0:T(8,128)(2,1)} %bitcast.9, ...), custom_call_target="tpu_custom_call" | custom-call | tf_op jit(solution)/shard_map/attention/pallas_call | solution.py:224
  2.2 0.0 copy-start.3
  2.2 27.4 %all_to_all.40 = bf16[16,2,1152]{2,1,0:T(2,128)(2,1)S(1)} all-to-all(bf16[16,2,1152]{2,1,0:T(2,128)(2,1)S(1)} %broadcast_in_dim.9), channel_id=1, replica_groups=mesh['side'=2,'yhi'=2,'zq'=8,'zp'=2,'x'=4,'core'=2] {'zq','zp'}, dimensions={0} | all-to-all | bytes 147456 | tf_op jit(solution)/shard_map/all_to_all | solution.py:29
  29.6 0.0 copy-start
  29.7 0.0 copy-start.1
  29.7 9.7 %all_to_all.41 = bf16[4,32,1152]{2,1,0:T(8,128)(2,1)S(1)} all-to-all(bf16[4,32,1152]{2,1,0:T(8,128)(2,1)S(1)} %broadcast_in_dim.10), channel_id=1, replica_groups=mesh['side'=2,'yhi'=2,'zq'=8,'zp'=2,'x'=4,'core'=2] {'side','yhi'}, dimensions={0} | all-to-all | bytes 589824 | tf_op jit(solution)/shard_map/all_to_all | solution.py:29
  39.4 0.0 copy-done.3
  39.4 0.4 project.1
  39.9 13.1 %all_to_all.42.parts_ref = bf16[8,64,128]{2,1,0:T(8,128)(2,1)S(1)} all-to-all(bf16[8,64,128]{2,1,0:T(8,128)(2,1)S(1)} %project.1), channel_id=1, replica_groups=mesh['side'=2,'yhi'=2,'zq'=8,'zp'=2,'x'=4,'core'=2] {'x','core'}, dimensions={0} | all-to-all | bytes 262144 | tf_op jit(solution)/shard_map/all_to_all | solution.py:260
  53.0 0.0 copy-done
  53.0 0.0 copy-done.1
  53.0 0.4 gate_up.1
  53.4 15.6 %all_to_all.43.parts_ref = bf16[8,8,7296]{2,1,0:T(8,128)(2,1)S(1)} all-to-all(bf16[8,8,7296]{2,1,0:T(8,128)(2,1)S(1)} %get-tuple-element.14), channel_id=1, replica_groups=mesh['side'=2,'yhi'=2,'zq'=8,'zp'=2,'x'=4,'core'=2] {'side','yhi','zp'}, dimensions={0} | all-to-all | bytes 1867776 | tf_op jit(solution)/shard_map/all_to_all | solution.py:269
  69.0 0.3 near_sum.1
  69.3 16.2 %all_to_all.44.parts_ref = bf16[8,4,1920]{2,1,0:T(4,128)(2,1)S(1)} all-to-all(bf16[8,4,1920]{2,1,0:T(4,128)(2,1)S(1)} %near_sum.1), channel_id=1, replica_groups=mesh['side'=2,'yhi'=2,'zq'=8,'zp'=2,'x'=4,'core'=2] {'zq'}, dimensions={0} | all-to-all | bytes 245760 | tf_op jit(solution)/shard_map/all_to_all | solution.py:278
  85.5 0.2 activate.1
  85.7 14.5 %all_to_all.45 = bf16[16,4,896]{2,1,0:T(4,128)(2,1)S(1)} all-to-all(bf16[16,4,896]{2,1,0:T(4,128)(2,1)S(1)} %activate.1), channel_id=1, replica_groups=mesh['side'=2,'yhi'=2,'zq'=8,'zp'=2,'x'=4,'core'=2] {'zq','zp'}, dimensions={0} | all-to-all | bytes 229376 | tf_op jit(solution)/shard_map/all_to_all | solution.py:287
  100.1 0.0 copy-start.2
  100.2 8.9 %all_to_all.46.active_ref = bf16[4,64,896]{2,1,0:T(8,128)(2,1)S(1)} all-to-all(bf16[4,64,896]{2,1,0:T(8,128)(2,1)S(1)} %broadcast_in_dim.11), channel_id=1, replica_groups=mesh['side'=2,'yhi'=2,'zq'=8,'zp'=2,'x'=4,'core'=2] {'side','yhi'}, dimensions={0} | all-to-all | bytes 917504 | tf_op jit(solution)/shard_map/all_to_all | solution.py:29
  109.1 0.0 copy-done.2
  109.1 0.3 down.1
  109.5 13.9 %all_to_all.47 = bf16[8,64,128]{2,1,0:T(8,128)(2,1)S(1)} all-to-all(bf16[8,64,128]{2,1,0:T(8,128)(2,1)S(1)} %down.1), channel_id=1, replica_groups=mesh['side'=2,'yhi'=2,'zq'=8,'zp'=2,'x'=4,'core'=2] {'x','core'}, dimensions={0} | all-to-all | bytes 262144 | tf_op jit(solution)/shard_map/all_to_all | solution.py:297
  123.4 0.6 add_convert_fusion
  (6 shorter events, 0.2 us)
Async XLA Ops:
  2.2 37.2 %copy-start.3 = (bf16[1024,128]{1,0:T(8,128)(2,1)S(1)}, bf16[1024,128]{1,0:T(8,128)(2,1)}, u32[]{:S(2)}) copy-start(bf16[1024,128]{1,0:T(8,128)(2,1)} %weight_ref.2) | copy-start | bytes 786436
  29.6 23.4 %copy-start = (bf16[128,3584]{1,0:T(8,128)(2,1)S(1)}, bf16[128,3584]{1,0:T(8,128)(2,1)}, u32[]{:S(2)}) copy-start(bf16[128,3584]{1,0:T(8,128)(2,1)} %gate_ref.1) | copy-start | bytes 2752516
  29.7 23.4 %copy-start.1 = (bf16[128,3584]{1,0:T(8,128)(2,1)S(1)}, bf16[128,3584]{1,0:T(8,128)(2,1)}, u32[]{:S(2)}) copy-start(bf16[128,3584]{1,0:T(8,128)(2,1)} %up_ref.1) | copy-start | bytes 2752516
  100.1 9.0 %copy-start.2 = (bf16[3584,128]{1,0:T(8,128)(2,1)S(1)}, bf16[3584,128]{1,0:T(8,128)(2,1)}, u32[]{:S(2)}) copy-start(bf16[3584,128]{1,0:T(8,128)(2,1)} %weight_ref.3) | copy-start | bytes 2752516

commit v5 on v4

--- a/solution.py
+++ b/solution.py
@@ -23,6 +23,18 @@
 NEAR = ("side", "yhi", "zp")
 GY = ("x", "core")
 GYS = 8
+
+
+def order_far():
+    return [0, 4, 2, 6, 1, 5, 3, 7]
+
+
+def exchange_far(value):
+    return lax.all_to_all(value, "zq", 0, 0, axis_index_groups=[order_far()])
+
+
+def exchange_z(value):
+    return lax.all_to_all(value, Z, 0, 0, axis_index_groups=[[q * ZP + p for q in order_far() for p in range(ZP)]])
 
 
 def spread(value, axes, count):
@@ -275,7 +287,7 @@
         name="near_sum",
         compiler_params=SMALL,
     )(terms)
-    terms = lax.all_to_all(terms, "zq", 0, 0)
+    terms = exchange_far(terms)
     activated = pl.pallas_call(
         activate_kernel,
         out_shape=shape((ZS, step, part), bf16),
@@ -284,7 +296,7 @@
         name="activate",
         compiler_params=SMALL,
     )(terms)
-    along_z = lax.all_to_all(activated, Z, 0, 0).reshape(rows, part)
+    along_z = exchange_z(activated).reshape(rows, part)
     along_y = spread(along_z, Y, YS)
     ffn_parts = pl.pallas_call(
         down_kernel,

time: 124 us -> 124 us (level)
  no operation moved by 1% of the time
where the time goes in v5:
time: 124 us
  blocking collectives  119 us (96%)
  Pallas kernels  3.15 us (3%)
    all_to_all x3, blocking collectives, spread(): lax.all_to_all(jnp.broadcast_to(value, (count, *value.shape)), axes, 0, 0)  46 us
    all_to_all x1, blocking collectives, exchange_z(): lax.all_to_all(value, Z, 0, 0, axis_index_groups=[[q * ZP + p for q in or...  16.5 us
    all_to_all x1, blocking collectives, local(): terms = lax.all_to_all(terms, NEAR, 0, 0)  15.6 us
    all_to_all x1, blocking collectives, exchange_far(): return lax.all_to_all(value, 'zq', 0, 0, axis_index_groups=[order_far()])  14.4 us
    all_to_all x1, blocking collectives, local(): ffn_sum = jnp.sum(lax.all_to_all(ffn_parts, GY, 0, 0).astype(f32), axis=0)  13.5 us
    all_to_all x1, blocking collectives, local(): head_parts = lax.all_to_all(head_parts, GY, 0, 0)  13.1 us

profile of v5, /device:TPU:1, one launch (start us, length us, event | category | flops | bytes accessed | tf_op | source)
XLA Modules:
  0.0 123.9 jit_solution(14013113676263620919)
XLA Ops:
  0.7 1.5 %attention.1 = (bf16[2,1152]{1,0:T(2,128)(2,1)S(1)}, bf16[64,128]{1,0:T(8,128)(2,1)S(1)}, f32[1,128]{1,0:T(1,128)S(1)}) custom-call(s32[1]{0:T(128)S(6)} %copy.11.length_ref, bf16[16,128]{1,0:T(8,128)(2,1)} %bitcast.10, bf16[1024,256]{1,0:T(8,128)(2,1)} %bitcast.8, bf16[2,256]{1,0:T(2,128)(2,1)} %bitcast.11, bf16[64,128]{1,0:T(8,128)(2,1)} %bitcast.9, ...), custom_call_target="tpu_custom_call" | custom-call | tf_op jit(solution)/shard_map/attention/pallas_call | solution.py:236
  2.2 0.0 copy-start.3
  2.2 27.4 %all_to_all.40 = bf16[16,2,1152]{2,1,0:T(2,128)(2,1)S(1)} all-to-all(bf16[16,2,1152]{2,1,0:T(2,128)(2,1)S(1)} %broadcast_in_dim.9), channel_id=1, replica_groups=mesh['side'=2,'yhi'=2,'zq'=8,'zp'=2,'x'=4,'core'=2] {'zq','zp'}, dimensions={0} | all-to-all | bytes 147456 | tf_op jit(solution)/shard_map/all_to_all | solution.py:41
  29.6 0.0 copy-start
  29.7 0.0 copy-start.1
  29.7 9.7 %all_to_all.41 = bf16[4,32,1152]{2,1,0:T(8,128)(2,1)S(1)} all-to-all(bf16[4,32,1152]{2,1,0:T(8,128)(2,1)S(1)} %broadcast_in_dim.10), channel_id=1, replica_groups=mesh['side'=2,'yhi'=2,'zq'=8,'zp'=2,'x'=4,'core'=2] {'side','yhi'}, dimensions={0} | all-to-all | bytes 589824 | tf_op jit(solution)/shard_map/all_to_all | solution.py:41
  39.4 0.0 copy-done.3
  39.4 0.4 project.1
  39.9 13.1 %all_to_all.42.parts_ref = bf16[8,64,128]{2,1,0:T(8,128)(2,1)S(1)} all-to-all(bf16[8,64,128]{2,1,0:T(8,128)(2,1)S(1)} %project.1), channel_id=1, replica_groups=mesh['side'=2,'yhi'=2,'zq'=8,'zp'=2,'x'=4,'core'=2] {'x','core'}, dimensions={0} | all-to-all | bytes 262144 | tf_op jit(solution)/shard_map/all_to_all | solution.py:272
  53.0 0.0 copy-done
  53.0 0.0 copy-done.1
  53.0 0.4 gate_up.1
  53.4 15.6 %all_to_all.43.parts_ref = bf16[8,8,7296]{2,1,0:T(8,128)(2,1)S(1)} all-to-all(bf16[8,8,7296]{2,1,0:T(8,128)(2,1)S(1)} %get-tuple-element.14), channel_id=1, replica_groups=mesh['side'=2,'yhi'=2,'zq'=8,'zp'=2,'x'=4,'core'=2] {'side','yhi','zp'}, dimensions={0} | all-to-all | bytes 1867776 | tf_op jit(solution)/shard_map/all_to_all | solution.py:281
  69.0 0.3 near_sum.1
  69.3 14.4 %all_to_all.44.parts_ref = bf16[8,4,1920]{2,1,0:T(4,128)(2,1)S(1)} all-to-all(bf16[8,4,1920]{2,1,0:T(4,128)(2,1)S(1)} %near_sum.1), channel_id=1, replica_groups={{0,64,32,96,16,80,48,112},{1,65,33,97,17,81,49,113},{2,66,34,98,18,82,5..., dimensions={0} | all-to-all | bytes 245760 | tf_op jit(solution)/shard_map/all_to_all | solution.py:33
  83.7 0.2 activate.1
  83.9 16.5 %all_to_all.45 = bf16[16,4,896]{2,1,0:T(4,128)(2,1)S(1)} all-to-all(bf16[16,4,896]{2,1,0:T(4,128)(2,1)S(1)} %activate.1), channel_id=1, replica_groups={{0,8,64,72,32,40,96,104,16,24,80,88,48,56,112,120},{1,9,65,73,33,41,97,..., dimensions={0} | all-to-all | bytes 229376 | tf_op jit(solution)/shard_map/all_to_all | solution.py:37
  100.4 0.0 copy-start.2
  100.5 8.9 %all_to_all.46.active_ref = bf16[4,64,896]{2,1,0:T(8,128)(2,1)S(1)} all-to-all(bf16[4,64,896]{2,1,0:T(8,128)(2,1)S(1)} %broadcast_in_dim.11), channel_id=1, replica_groups=mesh['side'=2,'yhi'=2,'zq'=8,'zp'=2,'x'=4,'core'=2] {'side','yhi'}, dimensions={0} | all-to-all | bytes 917504 | tf_op jit(solution)/shard_map/all_to_all | solution.py:41
  109.4 0.0 copy-done.2
  109.4 0.3 down.1
  109.7 13.5 %all_to_all.47 = bf16[8,64,128]{2,1,0:T(8,128)(2,1)S(1)} all-to-all(bf16[8,64,128]{2,1,0:T(8,128)(2,1)S(1)} %down.1), channel_id=1, replica_groups=mesh['side'=2,'yhi'=2,'zq'=8,'zp'=2,'x'=4,'core'=2] {'x','core'}, dimensions={0} | all-to-all | bytes 262144 | tf_op jit(solution)/shard_map/all_to_all | solution.py:309
  123.2 0.6 add_convert_fusion
  (6 shorter events, 0.2 us)
Async XLA Ops:
  2.2 37.2 %copy-start.3 = (bf16[1024,128]{1,0:T(8,128)(2,1)S(1)}, bf16[1024,128]{1,0:T(8,128)(2,1)}, u32[]{:S(2)}) copy-start(bf16[1024,128]{1,0:T(8,128)(2,1)} %weight_ref.2) | copy-start | bytes 786436
  29.6 23.4 %copy-start = (bf16[128,3584]{1,0:T(8,128)(2,1)S(1)}, bf16[128,3584]{1,0:T(8,128)(2,1)}, u32[]{:S(2)}) copy-start(bf16[128,3584]{1,0:T(8,128)(2,1)} %gate_ref.1) | copy-start | bytes 2752516
  29.7 23.4 %copy-start.1 = (bf16[128,3584]{1,0:T(8,128)(2,1)S(1)}, bf16[128,3584]{1,0:T(8,128)(2,1)}, u32[]{:S(2)}) copy-start(bf16[128,3584]{1,0:T(8,128)(2,1)} %up_ref.1) | copy-start | bytes 2752516
  100.4 9.0 %copy-start.2 = (bf16[3584,128]{1,0:T(8,128)(2,1)S(1)}, bf16[3584,128]{1,0:T(8,128)(2,1)}, u32[]{:S(2)}) copy-start(bf16[3584,128]{1,0:T(8,128)(2,1)} %weight_ref.3) | copy-start | bytes 2752516

commit v6 on v5

--- a/solution.py
+++ b/solution.py
@@ -20,7 +20,7 @@
 ROWS = ("side", "yhi", "zq", "zp")
 Y = ("side", "yhi")
 Z = ("zq", "zp")
-NEAR = ("side", "yhi", "zp")
+NEAR = ("zp", "side", "yhi")
 GY = ("x", "core")
 GYS = 8
 
@@ -169,7 +169,7 @@
             block = slice((p * count + g) * tall, (p * count + g + 1) * tall)
             stats = jnp.where(lane == 2 * g, high[block], jnp.where(lane == 2 * g + 1, low[block], stats))
         for y in range(YS):
-            out_ref[y * ZP + p, :, 2 * part * count :] = stats.astype(bf16)
+            out_ref[p * YS + y, :, 2 * part * count :] = stats.astype(bf16)
     for y in range(YS):
         columns = slice(y * part, (y + 1) * part)
         for start, ref in ((0, gate_ref), (part, up_ref)):
@@ -177,7 +177,7 @@
             for p in range(ZP):
                 for g in range(count):
                     block = term[(p * count + g) * tall : (p * count + g + 1) * tall].astype(bf16)
-                    out_ref[y * ZP + p, :, 2 * part * g + start : 2 * part * g + start + part] = block
+                    out_ref[p * YS + y, :, 2 * part * g + start : 2 * part * g + start + part] = block
 
 
 def sum_kernel(parts_ref, out_ref):

time: 124 us -> 125 us (level)
  no operation moved by 1% of the time
where the time goes in v6:
time: 125 us; the launch traced here: 124 us
  blocking collectives  119 us (95%)
  Pallas kernels  3.15 us (3%)
    all_to_all x3, blocking collectives, spread(): lax.all_to_all(jnp.broadcast_to(value, (count, *value.shape)), axes, 0, 0)  46.4 us
    all_to_all x1, blocking collectives, exchange_z(): lax.all_to_all(value, Z, 0, 0, axis_index_groups=[[q * ZP + p for q in or...  16.4 us
    all_to_all x1, blocking collectives, local(): terms = lax.all_to_all(terms, NEAR, 0, 0)  15.5 us
    all_to_all x1, blocking collectives, exchange_far(): return lax.all_to_all(value, 'zq', 0, 0, axis_index_groups=[order_far()])  14.3 us
    all_to_all x1, blocking collectives, local(): ffn_sum = jnp.sum(lax.all_to_all(ffn_parts, GY, 0, 0).astype(f32), axis=0)  13.7 us
    all_to_all x1, blocking collectives, local(): head_parts = lax.all_to_all(head_parts, GY, 0, 0)  13.1 us

profile of v6, /device:TPU:1, one launch (start us, length us, event | category | flops | bytes accessed | tf_op | source)
XLA Modules:
  0.0 124.2 jit_solution(14909745000048568225)
XLA Ops:
  0.7 1.5 %attention.1 = (bf16[2,1152]{1,0:T(2,128)(2,1)S(1)}, bf16[64,128]{1,0:T(8,128)(2,1)S(1)}, f32[1,128]{1,0:T(1,128)S(1)}) custom-call(s32[1]{0:T(128)S(6)} %copy.11.length_ref, bf16[16,128]{1,0:T(8,128)(2,1)} %bitcast.10, bf16[1024,256]{1,0:T(8,128)(2,1)} %bitcast.8, bf16[2,256]{1,0:T(2,128)(2,1)} %bitcast.11, bf16[64,128]{1,0:T(8,128)(2,1)} %bitcast.9, ...), custom_call_target="tpu_custom_call" | custom-call | tf_op jit(solution)/shard_map/attention/pallas_call | solution.py:236
  2.2 0.0 copy-start.3
  2.2 27.4 %all_to_all.40 = bf16[16,2,1152]{2,1,0:T(2,128)(2,1)S(1)} all-to-all(bf16[16,2,1152]{2,1,0:T(2,128)(2,1)S(1)} %broadcast_in_dim.9), channel_id=1, replica_groups=mesh['side'=2,'yhi'=2,'zq'=8,'zp'=2,'x'=4,'core'=2] {'zq','zp'}, dimensions={0} | all-to-all | bytes 147456 | tf_op jit(solution)/shard_map/all_to_all | solution.py:41
  29.6 0.0 copy-start
  29.7 0.0 copy-start.1
  29.7 9.7 %all_to_all.41 = bf16[4,32,1152]{2,1,0:T(8,128)(2,1)S(1)} all-to-all(bf16[4,32,1152]{2,1,0:T(8,128)(2,1)S(1)} %broadcast_in_dim.10), channel_id=1, replica_groups=mesh['side'=2,'yhi'=2,'zq'=8,'zp'=2,'x'=4,'core'=2] {'side','yhi'}, dimensions={0} | all-to-all | bytes 589824 | tf_op jit(solution)/shard_map/all_to_all | solution.py:41
  39.4 0.0 copy-done.3
  39.4 0.4 project.1
  39.9 13.1 %all_to_all.42.parts_ref = bf16[8,64,128]{2,1,0:T(8,128)(2,1)S(1)} all-to-all(bf16[8,64,128]{2,1,0:T(8,128)(2,1)S(1)} %project.1), channel_id=1, replica_groups=mesh['side'=2,'yhi'=2,'zq'=8,'zp'=2,'x'=4,'core'=2] {'x','core'}, dimensions={0} | all-to-all | bytes 262144 | tf_op jit(solution)/shard_map/all_to_all | solution.py:272
  53.0 0.0 copy-done
  53.0 0.0 copy-done.1
  53.0 0.4 gate_up.1
  53.4 15.5 %all_to_all.43.parts_ref = bf16[8,8,7296]{2,1,0:T(8,128)(2,1)S(1)} all-to-all(bf16[8,8,7296]{2,1,0:T(8,128)(2,1)S(1)} %get-tuple-element.14), channel_id=1, replica_groups=mesh['side'=2,'yhi'=2,'zq'=8,'zp'=2,'x'=4,'core'=2] {'zp','side','yhi'}, dimensions={0} | all-to-all | bytes 1867776 | tf_op jit(solution)/shard_map/all_to_all | solution.py:281
  68.9 0.3 near_sum.1
  69.2 14.3 %all_to_all.44.parts_ref = bf16[8,4,1920]{2,1,0:T(4,128)(2,1)S(1)} all-to-all(bf16[8,4,1920]{2,1,0:T(4,128)(2,1)S(1)} %near_sum.1), channel_id=1, replica_groups={{0,64,32,96,16,80,48,112},{1,65,33,97,17,81,49,113},{2,66,34,98,18,82,5..., dimensions={0} | all-to-all | bytes 245760 | tf_op jit(solution)/shard_map/all_to_all | solution.py:33
  83.6 0.2 activate.1
  83.8 16.4 %all_to_all.45 = bf16[16,4,896]{2,1,0:T(4,128)(2,1)S(1)} all-to-all(bf16[16,4,896]{2,1,0:T(4,128)(2,1)S(1)} %activate.1), channel_id=1, replica_groups={{0,8,64,72,32,40,96,104,16,24,80,88,48,56,112,120},{1,9,65,73,33,41,97,..., dimensions={0} | all-to-all | bytes 229376 | tf_op jit(solution)/shard_map/all_to_all | solution.py:37
  100.1 0.0 copy-start.2
  100.2 9.3 %all_to_all.46.active_ref = bf16[4,64,896]{2,1,0:T(8,128)(2,1)S(1)} all-to-all(bf16[4,64,896]{2,1,0:T(8,128)(2,1)S(1)} %broadcast_in_dim.11), channel_id=1, replica_groups=mesh['side'=2,'yhi'=2,'zq'=8,'zp'=2,'x'=4,'core'=2] {'side','yhi'}, dimensions={0} | all-to-all | bytes 917504 | tf_op jit(solution)/shard_map/all_to_all | solution.py:41
  109.5 0.0 copy-done.2
  109.5 0.3 down.1
  109.8 13.7 %all_to_all.47 = bf16[8,64,128]{2,1,0:T(8,128)(2,1)S(1)} all-to-all(bf16[8,64,128]{2,1,0:T(8,128)(2,1)S(1)} %down.1), channel_id=1, replica_groups=mesh['side'=2,'yhi'=2,'zq'=8,'zp'=2,'x'=4,'core'=2] {'x','core'}, dimensions={0} | all-to-all | bytes 262144 | tf_op jit(solution)/shard_map/all_to_all | solution.py:309
  123.6 0.6 add_convert_fusion
  (6 shorter events, 0.2 us)
Async XLA Ops:
  2.2 37.2 %copy-start.3 = (bf16[1024,128]{1,0:T(8,128)(2,1)S(1)}, bf16[1024,128]{1,0:T(8,128)(2,1)}, u32[]{:S(2)}) copy-start(bf16[1024,128]{1,0:T(8,128)(2,1)} %weight_ref.2) | copy-start | bytes 786436
  29.6 23.4 %copy-start = (bf16[128,3584]{1,0:T(8,128)(2,1)S(1)}, bf16[128,3584]{1,0:T(8,128)(2,1)}, u32[]{:S(2)}) copy-start(bf16[128,3584]{1,0:T(8,128)(2,1)} %gate_ref.1) | copy-start | bytes 2752516
  29.7 23.4 %copy-start.1 = (bf16[128,3584]{1,0:T(8,128)(2,1)S(1)}, bf16[128,3584]{1,0:T(8,128)(2,1)}, u32[]{:S(2)}) copy-start(bf16[128,3584]{1,0:T(8,128)(2,1)} %up_ref.1) | copy-start | bytes 2752516
  100.1 9.3 %copy-start.2 = (bf16[3584,128]{1,0:T(8,128)(2,1)S(1)}, bf16[3584,128]{1,0:T(8,128)(2,1)}, u32[]{:S(2)}) copy-start(bf16[3584,128]{1,0:T(8,128)(2,1)} %weight_ref.3) | copy-start | bytes 2752516
